TPU v7x, 32 devices: a whole 2x2x4 slice. The times are simulated.
32 devices in a mesh: pipe: 4 (over y, x), seq: 8 (over z, core).
Axes of the slice: x: 2, y: 2, z: 4, core: 2. Of those that a mesh axis runs over, the one named last changes fastest.
Arguments:
- query_rows: bfloat16 [4, 1024, 1536], P('pipe', 'seq'), may hold values from -6 to 6
- key_rows: bfloat16 [4, 1024, 1536], P('pipe', 'seq'), may hold values from -6 to 6
- value_rows: bfloat16 [4, 1024, 1536], P('pipe', 'seq'), may hold values from -6 to 6
- query_weight: bfloat16 [4, 1536, 1536], P('pipe'), may hold values from -0.15625 to 0.15625
- key_weight: bfloat16 [4, 1536, 1536], P('pipe'), may hold values from -0.15625 to 0.15625
- value_weight: bfloat16 [4, 1536, 1536], P('pipe'), may hold values from -0.15625 to 0.15625
- out_weight: bfloat16 [4, 1536, 1536], P('pipe'), may hold values from -0.15625 to 0.15625
- upstream: bfloat16 [1024, 1536], P('seq'), may hold values from -6 to 6
- window: int32 [8, 12, 2], replicated, may hold values from 0 to 1, as said below
Outputs:
- gradients: bfloat16 [4, 1024, 1536], P('pipe', 'seq')
Inputs may be any that keep to these rules, and one draw needn't show every extreme that they name: window[i, h, 0] is 0 where i % 4 == 3, and window[i, h, 1] is 0 where i % 4 == 2.
All inputs are finite; a program needn't handle non-finite values.
Results may differ from a plain program's by a relative error of at most 0.02.
Values may be sent and summed in bfloat16 or wider, within the bound.
No kernel may reach another device: no remote copies, remote signals or barrier semaphores. Data moves between devices by JAX's collectives and lax.ppermute only.
A program may use at most 128 MiB of HBM per device.

v0:
```python
import functools

import jax
import jax.numpy as jnp
from jax import lax
from jax.experimental import pallas as pl
from jax.experimental.pallas import tpu as pltpu
from jax.sharding import PartitionSpec as P

HEAD_DIM = 128
TILE = 128
MIB = 1 << 20


def dot_nt(a, b):
    return lax.dot_general(a, b, (((1,), (1,)), ((), ())), preferred_element_type=jnp.float32)


def dot_nn(a, b):
    return lax.dot_general(a, b, (((1,), (0,)), ((), ())), preferred_element_type=jnp.float32)


def prob_kernel(heads, scaling, flags, q_ref, k0_ref, k1_ref, k2_ref, pt_ref, kt_ref):
    for h in range(heads):
        cols = pl.ds(h * HEAD_DIM, HEAD_DIM)
        q = q_ref[:, cols]
        scores = []
        for b, k_ref in enumerate((k0_ref, k1_ref, k2_ref)):
            k = k_ref[:, cols]
            s = scaling * dot_nt(k, q)
            if b > 0:
                s = jnp.where(flags[b - 1, h] > 0, s, -jnp.inf)
            scores.append(s)
            kt_ref[h, :, pl.ds(b * TILE, TILE)] = k.T
        top = jnp.maximum(jnp.maximum(scores[0], scores[1]), scores[2])
        top = jnp.max(top, axis=0, keepdims=True)
        weights = [jnp.exp(s - top) for s in scores]
        total = jnp.sum(weights[0] + weights[1] + weights[2], axis=0, keepdims=True)
        scale = 1.0 / total
        for b, w in enumerate(weights):
            pt_ref[h, pl.ds(b * TILE, TILE), :] = (w * scale).astype(jnp.bfloat16)


def stage_kernel(
    heads,
    scaling,
    x_ref,
    q_ref,
    v0_ref,
    v1_ref,
    v2_ref,
    pt_ref,
    kt_ref,
    wo_hbm,
    wq_hbm,
    wk_hbm,
    wv_hbm,
    own_ref,
    core_ref,
    far_ref,
    wo,
    wq,
    wk,
    wv,
    dq,
    dk,
    dv,
    sems,
):
    width = wo.shape[0]
    groups = 4
    rows = width // groups
    out_copies = []
    for g in range(groups):
        part = pl.ds(g * rows, rows)
        out_copies.append(pltpu.make_async_copy(wo_hbm.at[part], wo.at[part], sems.at[g]))
    others = [
        pltpu.make_async_copy(src, dst, sems.at[groups + n])
        for n, (src, dst) in enumerate(((wk_hbm, wk), (wv_hbm, wv), (wq_hbm, wq)))
    ]
    for copy in out_copies + others:
        copy.start()
    x = x_ref[...]
    per = heads // groups
    for g in range(groups):
        out_copies[g].wait()
        d_out = dot_nt(x, wo[pl.ds(g * rows, rows), :]).astype(jnp.bfloat16)
        for n in range(per):
            h = g * per + n
            cols = pl.ds(h * HEAD_DIM, HEAD_DIM)
            dh = d_out[:, n * HEAD_DIM : (n + 1) * HEAD_DIM]
            p = [pt_ref[h, pl.ds(b * TILE, TILE), :] for b in range(3)]
            pf = [t.astype(jnp.float32) for t in p]
            dp = [dot_nt(v_ref[:, cols], dh) for v_ref in (v0_ref, v1_ref, v2_ref)]
            prod = [a * b for a, b in zip(pf, dp)]
            delta = jnp.sum(prod[0] + prod[1] + prod[2], axis=0, keepdims=True)
            ds = [(a * ((b - delta) * scaling)).astype(jnp.bfloat16) for a, b in zip(pf, dp)]
            ds_all = jnp.concatenate(ds, axis=0)
            dq_t = dot_nn(kt_ref[h], ds_all)
            dq[:, cols] = dq_t.T.astype(jnp.bfloat16)
            dk[:, cols] = dot_nn(ds_all, q_ref[:, cols]).astype(jnp.bfloat16)
            dv[:, cols] = dot_nn(pt_ref[h], dh).astype(jnp.bfloat16)
    for copy in others:
        copy.wait()
    step = 512
    for n in range(own_ref.shape[1] // step):
        part = pl.ds(n * step, step)
        cross = dot_nt(dk[...], wk[part, :]) + dot_nt(dv[...], wv[part, :])
        own = cross[:TILE] + dot_nt(dq[...], wq[part, :]) + x_ref[:, part].astype(jnp.float32)
        own_ref[:, part] = own
        core_ref[:, part] = cross[TILE : 2 * TILE].astype(jnp.bfloat16)
        far_ref[:, part] = cross[2 * TILE :].astype(jnp.bfloat16)


def body(
    query_rows,
    key_rows,
    value_rows,
    query_weight,
    key_weight,
    value_weight,
    out_weight,
    upstream,
    window,
):
    sections = lax.axis_size("pipe")
    position = lax.axis_index("pipe")
    seq_size = lax.axis_size("seq")
    seq_index = lax.axis_index("seq")
    rows, width = query_rows.shape[1:]
    model = out_weight.shape[2]
    heads = width // HEAD_DIM
    scaling = HEAD_DIM ** (-0.5)
    near_pairs = [(i, i ^ 1) for i in range(seq_size)]
    far_pairs = [(i, i + 1) for i in range(1, seq_size - 1, 2)]
    far_pairs = far_pairs + [(j, i) for i, j in far_pairs]

    def near(value):
        return lax.ppermute(value, "seq", near_pairs)

    def far(value):
        return lax.ppermute(value, "seq", far_pairs)

    q, k, v = query_rows[0], key_rows[0], value_rows[0]
    k1, k2 = near(k), far(k)
    v1, v2 = near(v), far(v)
    flags = lax.dynamic_index_in_dim(window, seq_index, 0, keepdims=False)
    odd = seq_index % 2 == 1
    flags = jnp.where(
        odd,
        jnp.stack([flags[:, 0], flags[:, 1]]),
        jnp.stack([flags[:, 1], flags[:, 0]]),
    )
    vmem = pl.BlockSpec(memory_space=pltpu.VMEM)
    smem = pl.BlockSpec(memory_space=pltpu.SMEM)
    anywhere = pl.BlockSpec(memory_space=pl.ANY)
    bf16 = jnp.bfloat16
    pt, kt = pl.pallas_call(
        functools.partial(prob_kernel, heads, scaling),
        in_specs=[smem, vmem, vmem, vmem, vmem],
        out_specs=[vmem, vmem],
        out_shape=[
            jax.ShapeDtypeStruct((heads, 3 * TILE, rows), bf16),
            jax.ShapeDtypeStruct((heads, HEAD_DIM, 3 * TILE), bf16),
        ],
        compiler_params=pltpu.CompilerParams(vmem_limit_bytes=32 * MIB),
        name="prob",
    )(flags, q, k, k1, k2)

    stage = pl.pallas_call(
        functools.partial(stage_kernel, heads, scaling),
        in_specs=[vmem] * 7 + [anywhere] * 4,
        out_specs=[vmem] * 3,
        out_shape=[
            jax.ShapeDtypeStruct((rows, model), jnp.float32),
            jax.ShapeDtypeStruct((rows, model), bf16),
            jax.ShapeDtypeStruct((rows, model), bf16),
        ],
        scratch_shapes=[
            pltpu.VMEM((width, model), bf16),
            pltpu.VMEM((model, width), bf16),
            pltpu.VMEM((model, width), bf16),
            pltpu.VMEM((model, width), bf16),
            pltpu.VMEM((rows, width), bf16),
            pltpu.VMEM((3 * rows, width), bf16),
            pltpu.VMEM((3 * rows, width), bf16),
            pltpu.SemaphoreType.DMA((7,)),
        ],
        compiler_params=pltpu.CompilerParams(vmem_limit_bytes=48 * MIB),
        name="stage",
    )
    wo, wq, wk, wv = out_weight[0], query_weight[0], key_weight[0], value_weight[0]
    incoming = upstream
    result = jnp.zeros((rows, model), bf16)
    for step in range(sections):
        own, to_near, to_far = stage(incoming, q, v, v1, v2, pt, kt, wo, wq, wk, wv)
        from_far = far(to_far)
        from_near = near(to_near)
        finished = own + from_near.astype(jnp.float32) + from_far.astype(jnp.float32)
        finished = finished.astype(bf16)
        result = jnp.where(position == sections - 1 - step, finished, result)
        if step < sections - 1:
            source = sections - 1 - step
            incoming = lax.ppermute(finished, "pipe", [(source, source - 1)])
    return result[None]


def solution(mesh):
    in_specs = (
        P("pipe", "seq", None),
        P("pipe", "seq", None),
        P("pipe", "seq", None),
        P("pipe", None, None),
        P("pipe", None, None),
        P("pipe", None, None),
        P("pipe", None, None),
        P("seq", None),
        P(),
    )
    out_specs = P("pipe", "seq", None)
    return jax.shard_map(body, mesh=mesh, in_specs=in_specs, out_specs=out_specs, check_vma=False)
```

profile of v0, /device:TPU:1, one launch (start us, length us, event | category | flops | bytes accessed | tf_op | source)
XLA Modules:
  0.0 148.2 jit_solution(8477326093082009715)
XLA Ops:
  0.1 4.5 %collective-permute-start.3 = (bf16[128,1536]{1,0:T(8,128)(2,1)}, bf16[128,1536]{1,0:T(8,128)(2,1)S(1)}, u32[]{:S(2)}, u32[]{:S(2)}) collective-permute-start(bf16[128,1536]{1,0:T(8,128)(2,1)} %bitcast.27), channel_id=1, source_target_pairs={{1,2},{3,4},{5,6},{2,1},{4,3},{6,5},{9,10},{11,12},{13,14},{10,9},... | collective-permute-start | bytes 1179656 | tf_op jit(solution)/shard_map/ppermute | solution.py:142
  4.7 3.6 %collective-permute-start.1 = (bf16[128,1536]{1,0:T(8,128)(2,1)}, bf16[128,1536]{1,0:T(8,128)(2,1)S(1)}, u32[]{:S(2)}, u32[]{:S(2)}) collective-permute-start(bf16[128,1536]{1,0:T(8,128)(2,1)} %bitcast.21), channel_id=1, source_target_pairs={{1,2},{3,4},{5,6},{2,1},{4,3},{6,5},{9,10},{11,12},{13,14},{10,9},... | collective-permute-start | bytes 1179656 | tf_op jit(solution)/shard_map/ppermute | solution.py:142
  8.4 1.9 %collective-permute-done.3.k2_ref = bf16[128,1536]{1,0:T(8,128)(2,1)S(1)} collective-permute-done((bf16[128,1536]{1,0:T(8,128)(2,1)}, bf16[128,1536]{1,0:T(8,128)(2,1)S(1)}, u32[]{:S(2)}, u32[]{:S(2)}) %collective-permute-start.3) | collective-permute-done | bytes 393248 | tf_op jit(solution)/shard_map/ppermute | solution.py:142
  10.3 1.0 copy-done.1
  11.3 1.0 copy-done.5
  12.3 1.8 %prob.1 = (bf16[12,384,128]{2,1,0:T(8,128)(2,1)S(1)}, bf16[12,128,384]{2,1,0:T(8,128)(2,1)S(1)}) custom-call(s32[2,12]{1,0:T(2,128)S(1)} %add_select_fusion.flags, bf16[128,1536]{1,0:T(8,128)(2,1)S(1)} %bitcast.15, bf16[128,1536]{1,0:T(8,128)(2,1)S(1)} %bitcast.28, bf16[128,1536]{1,0:T(8,128)(2,1)S(1)} %collective-permute-done.2.k1_ref, ...), custom_call_target="tpu_custom_call" | custom-call | tf_op jit(solution)/shard_map/prob/pallas_call | solution.py:158
  14.5 1.0 copy-done.2
  15.5 1.0 copy-done.3
  16.5 1.0 copy-done.6
  17.5 13.5 %stage.4 = (f32[128,1536]{1,0:T(8,128)S(1)}, bf16[128,1536]{1,0:T(8,128)(2,1)S(1)}, bf16[128,1536]{1,0:T(8,128)(2,1)S(1)}) custom-call(bf16[128,1536]{1,0:T(8,128)(2,1)S(1)} %copy-done.6, bf16[128,1536]{1,0:T(8,128)(2,1)S(1)} %bitcast.16, bf16[128,1536]{1,0:T(8,128)(2,1)S(1)} %bitcast.22, bf16[128,1536]{1,0:T(8,128)(2,1)S(1)} %collective-permute-done.v1_ref, ...), custom_call_target="tpu_custom_call" | custom-call | tf_op jit(solution)/shard_map/stage/pallas_call | solution.py:196
  31.1 4.1 %collective-permute-start.5 = (bf16[128,1536]{1,0:T(8,128)(2,1)S(1)}, bf16[128,1536]{1,0:T(8,128)(2,1)S(1)}, u32[]{:S(2)}, u32[]{:S(2)}) collective-permute-start(bf16[128,1536]{1,0:T(8,128)(2,1)S(1)} %get-tuple-element.23), channel_id=1, source_target_pairs={{1,2},{3,4},{5,6},{2,1},{4,3},{6,5},{9,10},{11,12},{13,14},{10,9},... | collective-permute-start | bytes 1179656 | tf_op jit(solution)/shard_map/ppermute | solution.py:142
  35.2 5.4 %collective-permute-done.5 = bf16[128,1536]{1,0:T(8,128)(2,1)S(1)} collective-permute-done((bf16[128,1536]{1,0:T(8,128)(2,1)S(1)}, bf16[128,1536]{1,0:T(8,128)(2,1)S(1)}, u32[]{:S(2)}, u32[]{:S(2)}) %collective-permute-start.5) | collective-permute-done | bytes 393248 | tf_op jit(solution)/shard_map/ppermute | solution.py:142
  41.7 13.5 %stage.5 = (f32[128,1536]{1,0:T(8,128)S(1)}, bf16[128,1536]{1,0:T(8,128)(2,1)S(1)}, bf16[128,1536]{1,0:T(8,128)(2,1)S(1)}) custom-call(bf16[128,1536]{1,0:T(8,128)(2,1)S(1)} %collective-permute-done.6.x_ref, bf16[128,1536]{1,0:T(8,128)(2,1)S(1)} %bitcast.17, bf16[128,1536]{1,0:T(8,128)(2,1)S(1)} %bitcast.23, ...), custom_call_target="tpu_custom_call" | custom-call | tf_op jit(solution)/shard_map/stage/pallas_call | solution.py:196
  55.2 3.7 %collective-permute-start.8 = (bf16[128,1536]{1,0:T(8,128)(2,1)S(1)}, bf16[128,1536]{1,0:T(8,128)(2,1)S(1)}, u32[]{:S(2)}, u32[]{:S(2)}) collective-permute-start(bf16[128,1536]{1,0:T(8,128)(2,1)S(1)} %get-tuple-element.26), channel_id=1, source_target_pairs={{1,2},{3,4},{5,6},{2,1},{4,3},{6,5},{9,10},{11,12},{13,14},{10,9},... | collective-permute-start | bytes 1179656 | tf_op jit(solution)/shard_map/ppermute | solution.py:142
  59.0 5.4 %collective-permute-done.8 = bf16[128,1536]{1,0:T(8,128)(2,1)S(1)} collective-permute-done((bf16[128,1536]{1,0:T(8,128)(2,1)S(1)}, bf16[128,1536]{1,0:T(8,128)(2,1)S(1)}, u32[]{:S(2)}, u32[]{:S(2)}) %collective-permute-start.8) | collective-permute-done | bytes 393248 | tf_op jit(solution)/shard_map/ppermute | solution.py:142
  65.5 13.5 %stage.6 = (f32[128,1536]{1,0:T(8,128)S(1)}, bf16[128,1536]{1,0:T(8,128)(2,1)S(1)}, bf16[128,1536]{1,0:T(8,128)(2,1)S(1)}) custom-call(bf16[128,1536]{1,0:T(8,128)(2,1)S(1)} %collective-permute-done.9.x_ref, bf16[128,1536]{1,0:T(8,128)(2,1)S(1)} %bitcast.18, bf16[128,1536]{1,0:T(8,128)(2,1)S(1)} %bitcast.24, ...), custom_call_target="tpu_custom_call" | custom-call | tf_op jit(solution)/shard_map/stage/pallas_call | solution.py:196
  79.0 4.0 %collective-permute-start.11 = (bf16[128,1536]{1,0:T(8,128)(2,1)S(1)}, bf16[128,1536]{1,0:T(8,128)(2,1)S(1)}, u32[]{:S(2)}, u32[]{:S(2)}) collective-permute-start(bf16[128,1536]{1,0:T(8,128)(2,1)S(1)} %get-tuple-element.29), channel_id=1, source_target_pairs={{1,2},{3,4},{5,6},{2,1},{4,3},{6,5},{9,10},{11,12},{13,14},{10,9},... | collective-permute-start | bytes 1179656 | tf_op jit(solution)/shard_map/ppermute | solution.py:142
  83.1 5.4 %collective-permute-done.11 = bf16[128,1536]{1,0:T(8,128)(2,1)S(1)} collective-permute-done((bf16[128,1536]{1,0:T(8,128)(2,1)S(1)}, bf16[128,1536]{1,0:T(8,128)(2,1)S(1)}, u32[]{:S(2)}, u32[]{:S(2)}) %collective-permute-start.11) | collective-permute-done | bytes 393248 | tf_op jit(solution)/shard_map/ppermute | solution.py:142
  88.7 1.6 %collective-permute-start.12 = (bf16[128,1536]{1,0:T(8,128)(2,1)S(1)}, bf16[128,1536]{1,0:T(8,128)(2,1)S(1)}, u32[]{:S(2)}, u32[]{:S(2)}) collective-permute-start(bf16[128,1536]{1,0:T(8,128)(2,1)S(1)} %add_convert_fusion.1), channel_id=1, source_target_pairs={{8,0},{9,1},{10,2},{11,3},{12,4},{13,5},{14,6},{15,7}} | collective-permute-start | bytes 1179656 | tf_op jit(solution)/shard_map/ppermute | solution.py:204
  90.2 29.4 %collective-permute-done.12.x_ref = bf16[128,1536]{1,0:T(8,128)(2,1)S(1)} collective-permute-done((bf16[128,1536]{1,0:T(8,128)(2,1)S(1)}, bf16[128,1536]{1,0:T(8,128)(2,1)S(1)}, u32[]{:S(2)}, u32[]{:S(2)}) %collective-permute-start.12) | collective-permute-done | bytes 393248 | tf_op jit(solution)/shard_map/ppermute | solution.py:204
  119.6 13.5 %stage.7 = (f32[128,1536]{1,0:T(8,128)S(1)}, bf16[128,1536]{1,0:T(8,128)(2,1)S(1)}, bf16[128,1536]{1,0:T(8,128)(2,1)S(1)}) custom-call(bf16[128,1536]{1,0:T(8,128)(2,1)S(1)} %collective-permute-done.12.x_ref, bf16[128,1536]{1,0:T(8,128)(2,1)S(1)} %bitcast.19, bf16[128,1536]{1,0:T(8,128)(2,1)S(1)} %bitcast.25, ...), custom_call_target="tpu_custom_call" | custom-call | tf_op jit(solution)/shard_map/stage/pallas_call | solution.py:196
  133.2 8.5 %collective-permute-start.14 = (bf16[128,1536]{1,0:T(8,128)(2,1)S(1)}, bf16[128,1536]{1,0:T(8,128)(2,1)S(1)}, u32[]{:S(2)}, u32[]{:S(2)}) collective-permute-start(bf16[128,1536]{1,0:T(8,128)(2,1)S(1)} %get-tuple-element.32), channel_id=1, source_target_pairs={{1,2},{3,4},{5,6},{2,1},{4,3},{6,5},{9,10},{11,12},{13,14},{10,9},... | collective-permute-start | bytes 1179656 | tf_op jit(solution)/shard_map/ppermute | solution.py:142
  141.7 5.4 %collective-permute-done.14 = bf16[128,1536]{1,0:T(8,128)(2,1)S(1)} collective-permute-done((bf16[128,1536]{1,0:T(8,128)(2,1)S(1)}, bf16[128,1536]{1,0:T(8,128)(2,1)S(1)}, u32[]{:S(2)}, u32[]{:S(2)}) %collective-permute-start.14) | collective-permute-done | bytes 393248 | tf_op jit(solution)/shard_map/ppermute | solution.py:142
  147.1 1.0 fusion.1
  (32 shorter events, 3.0 us)
Async XLA Ops:
  0.0 8.3 %copy-start = (s32[8,12,2]{1,2,0:T(2,128)S(1)}, s32[8,12,2]{1,2,0:T(2,128)}, u32[]{:S(2)}) copy-start(s32[8,12,2]{1,2,0:T(2,128)} %param.17) | copy-start | bytes 2308
  0.0 8.3 %collective-permute-start.2 = (bf16[128,1536]{1,0:T(8,128)(2,1)}, bf16[128,1536]{1,0:T(8,128)(2,1)S(1)}, u32[]{:S(2)}, u32[]{:S(2)}) collective-permute-start(bf16[128,1536]{1,0:T(8,128)(2,1)} %bitcast.26), channel_id=1, source_target_pairs={{0,1},{1,0},{2,3},{3,2},{4,5},{5,4},{6,7},{7,6},{8,9},{9,8},{10,11... | collective-permute-start | bytes 1179656 | tf_op jit(solution)/shard_map/ppermute | solution.py:139
  0.1 10.2 %collective-permute-start.3 = (bf16[128,1536]{1,0:T(8,128)(2,1)}, bf16[128,1536]{1,0:T(8,128)(2,1)S(1)}, u32[]{:S(2)}, u32[]{:S(2)}) collective-permute-start(bf16[128,1536]{1,0:T(8,128)(2,1)} %bitcast.27), channel_id=1, source_target_pairs={{1,2},{3,4},{5,6},{2,1},{4,3},{6,5},{9,10},{11,12},{13,14},{10,9},... | collective-permute-start | bytes 1179656 | tf_op jit(solution)/shard_map/ppermute | solution.py:142
  4.6 9.5 %collective-permute-start = (bf16[128,1536]{1,0:T(8,128)(2,1)}, bf16[128,1536]{1,0:T(8,128)(2,1)S(1)}, u32[]{:S(2)}, u32[]{:S(2)}) collective-permute-start(bf16[128,1536]{1,0:T(8,128)(2,1)} %bitcast.20), channel_id=1, source_target_pairs={{0,1},{1,0},{2,3},{3,2},{4,5},{5,4},{6,7},{7,6},{8,9},{9,8},{10,11... | collective-permute-start | bytes 1179656 | tf_op jit(solution)/shard_map/ppermute | solution.py:139
  4.7 9.8 %collective-permute-start.1 = (bf16[128,1536]{1,0:T(8,128)(2,1)}, bf16[128,1536]{1,0:T(8,128)(2,1)S(1)}, u32[]{:S(2)}, u32[]{:S(2)}) collective-permute-start(bf16[128,1536]{1,0:T(8,128)(2,1)} %bitcast.21), channel_id=1, source_target_pairs={{1,2},{3,4},{5,6},{2,1},{4,3},{6,5},{9,10},{11,12},{13,14},{10,9},... | collective-permute-start | bytes 1179656 | tf_op jit(solution)/shard_map/ppermute | solution.py:142
  10.3 1.0 copy-start.1
  11.3 1.0 copy-start.5
  14.5 1.0 copy-start.2
  15.5 1.0 copy-start.3
  16.5 1.0 copy-start.6
  17.5 24.2 %copy-start.4 = (bf16[1,128,1536]{2,1,0:T(8,128)(2,1)S(1)}, bf16[1,128,1536]{2,1,0:T(8,128)(2,1)}, u32[]{:S(2)}) copy-start(bf16[1,128,1536]{2,1,0:T(8,128)(2,1)} %param.11) | copy-start | bytes 1179652
  31.0 4.2 %collective-permute-start.4 = (bf16[128,1536]{1,0:T(8,128)(2,1)S(1)}, bf16[128,1536]{1,0:T(8,128)(2,1)S(1)}, u32[]{:S(2)}, u32[]{:S(2)}) collective-permute-start(bf16[128,1536]{1,0:T(8,128)(2,1)S(1)} %get-tuple-element.22), channel_id=1, source_target_pairs={{0,1},{1,0},{2,3},{3,2},{4,5},{5,4},{6,7},{7,6},{8,9},{9,8},{10,11... | collective-permute-start | bytes 1179656 | tf_op jit(solution)/shard_map/ppermute | solution.py:139
  31.1 9.6 %collective-permute-start.5 = (bf16[128,1536]{1,0:T(8,128)(2,1)S(1)}, bf16[128,1536]{1,0:T(8,128)(2,1)S(1)}, u32[]{:S(2)}, u32[]{:S(2)}) collective-permute-start(bf16[128,1536]{1,0:T(8,128)(2,1)S(1)} %get-tuple-element.23), channel_id=1, source_target_pairs={{1,2},{3,4},{5,6},{2,1},{4,3},{6,5},{9,10},{11,12},{13,14},{10,9},... | collective-permute-start | bytes 1179656 | tf_op jit(solution)/shard_map/ppermute | solution.py:142
  40.8 0.9 collective-permute-start.6
  55.1 3.8 %collective-permute-start.7 = (bf16[128,1536]{1,0:T(8,128)(2,1)S(1)}, bf16[128,1536]{1,0:T(8,128)(2,1)S(1)}, u32[]{:S(2)}, u32[]{:S(2)}) collective-permute-start(bf16[128,1536]{1,0:T(8,128)(2,1)S(1)} %get-tuple-element.25), channel_id=1, source_target_pairs={{0,1},{1,0},{2,3},{3,2},{4,5},{5,4},{6,7},{7,6},{8,9},{9,8},{10,11... | collective-permute-start | bytes 1179656 | tf_op jit(solution)/shard_map/ppermute | solution.py:139
  55.2 9.2 %collective-permute-start.8 = (bf16[128,1536]{1,0:T(8,128)(2,1)S(1)}, bf16[128,1536]{1,0:T(8,128)(2,1)S(1)}, u32[]{:S(2)}, u32[]{:S(2)}) collective-permute-start(bf16[128,1536]{1,0:T(8,128)(2,1)S(1)} %get-tuple-element.26), channel_id=1, source_target_pairs={{1,2},{3,4},{5,6},{2,1},{4,3},{6,5},{9,10},{11,12},{13,14},{10,9},... | collective-permute-start | bytes 1179656 | tf_op jit(solution)/shard_map/ppermute | solution.py:142
  64.6 0.9 collective-permute-start.9
  79.0 4.1 %collective-permute-start.10 = (bf16[128,1536]{1,0:T(8,128)(2,1)S(1)}, bf16[128,1536]{1,0:T(8,128)(2,1)S(1)}, u32[]{:S(2)}, u32[]{:S(2)}) collective-permute-start(bf16[128,1536]{1,0:T(8,128)(2,1)S(1)} %get-tuple-element.28), channel_id=1, source_target_pairs={{0,1},{1,0},{2,3},{3,2},{4,5},{5,4},{6,7},{7,6},{8,9},{9,8},{10,11... | collective-permute-start | bytes 1179656 | tf_op jit(solution)/shard_map/ppermute | solution.py:139
  79.0 9.5 %collective-permute-start.11 = (bf16[128,1536]{1,0:T(8,128)(2,1)S(1)}, bf16[128,1536]{1,0:T(8,128)(2,1)S(1)}, u32[]{:S(2)}, u32[]{:S(2)}) collective-permute-start(bf16[128,1536]{1,0:T(8,128)(2,1)S(1)} %get-tuple-element.29), channel_id=1, source_target_pairs={{1,2},{3,4},{5,6},{2,1},{4,3},{6,5},{9,10},{11,12},{13,14},{10,9},... | collective-permute-start | bytes 1179656 | tf_op jit(solution)/shard_map/ppermute | solution.py:142
  88.7 30.9 %collective-permute-start.12 = (bf16[128,1536]{1,0:T(8,128)(2,1)S(1)}, bf16[128,1536]{1,0:T(8,128)(2,1)S(1)}, u32[]{:S(2)}, u32[]{:S(2)}) collective-permute-start(bf16[128,1536]{1,0:T(8,128)(2,1)S(1)} %add_convert_fusion.1), channel_id=1, source_target_pairs={{8,0},{9,1},{10,2},{11,3},{12,4},{13,5},{14,6},{15,7}} | collective-permute-start | bytes 1179656 | tf_op jit(solution)/shard_map/ppermute | solution.py:204
  133.1 8.6 %collective-permute-start.13 = (bf16[128,1536]{1,0:T(8,128)(2,1)S(1)}, bf16[128,1536]{1,0:T(8,128)(2,1)S(1)}, u32[]{:S(2)}, u32[]{:S(2)}) collective-permute-start(bf16[128,1536]{1,0:T(8,128)(2,1)S(1)} %get-tuple-element.31), channel_id=1, source_target_pairs={{0,1},{1,0},{2,3},{3,2},{4,5},{5,4},{6,7},{7,6},{8,9},{9,8},{10,11... | collective-permute-start | bytes 1179656 | tf_op jit(solution)/shard_map/ppermute | solution.py:139
  133.2 14.0 %collective-permute-start.14 = (bf16[128,1536]{1,0:T(8,128)(2,1)S(1)}, bf16[128,1536]{1,0:T(8,128)(2,1)S(1)}, u32[]{:S(2)}, u32[]{:S(2)}) collective-permute-start(bf16[128,1536]{1,0:T(8,128)(2,1)S(1)} %get-tuple-element.32), channel_id=1, source_target_pairs={{1,2},{3,4},{5,6},{2,1},{4,3},{6,5},{9,10},{11,12},{13,14},{10,9},... | collective-permute-start | bytes 1179656 | tf_op jit(solution)/shard_map/ppermute | solution.py:142
where the time goes:
time: 149 us; the launch traced here: 148 us
  Pallas kernels  55.8 us (37%)
  waiting for transfers between devices  53.4 us (36%)
  starting transfers between devices  32.2 us (22%)
  local copies, waits for them, and re-layouts  5 us (3%)
    pallas_call x4, Pallas kernels, body(): own, to_near, to_far = stage(incoming, q, v, v1, v2, pt, kt, wo, wq, wk, wv)  53.9 us
    ppermute x3, waiting for transfers between devices, body(): incoming = lax.ppermute(finished, 'pipe', [(source, source - 1)])  29.4 us
    ppermute x6, starting transfers between devices, far(): return lax.ppermute(value, 'seq', far_pairs)  28.5 us
    ppermute x6, waiting for transfers between devices, far(): return lax.ppermute(value, 'seq', far_pairs)  24 us
    unnamed x14, local copies, waits for them, and re-layouts  4.99 us
    ppermute x3, starting transfers between devices, body(): incoming = lax.ppermute(finished, 'pipe', [(source, source - 1)])  3.33 us
  transfers between devices with their start and end apart: 15, of which 7 were waited for; matrix products, arithmetic and copies ran while one was open for 0% of the time, Pallas kernels for 1%

commit v1 on v0

v1 whole, which is shorter than its diff:
```python
import functools

import jax
import jax.numpy as jnp
from jax import lax
from jax.experimental import pallas as pl
from jax.experimental.pallas import tpu as pltpu
from jax.sharding import PartitionSpec as P

HEAD_DIM = 128
TILE = 128
MIB = 1 << 20


def dot_nt(a, b):
    return lax.dot_general(a, b, (((1,), (1,)), ((), ())), preferred_element_type=jnp.float32)


def dot_nn(a, b):
    return lax.dot_general(a, b, (((1,), (0,)), ((), ())), preferred_element_type=jnp.float32)


def pair_cols(g):
    return pl.ds(g * 2 * HEAD_DIM, 2 * HEAD_DIM)


def put_diagonal(target, g, value):
    target[g, pl.ds(0, TILE), pl.ds(0, HEAD_DIM)] = value[:, :HEAD_DIM]
    target[g, pl.ds(TILE, TILE), pl.ds(HEAD_DIM, HEAD_DIM)] = value[:, HEAD_DIM:]


def prep_kernel(
    wo_hbm, wq_hbm, wk_hbm, wv_hbm, q_hbm, k_hbm, v_hbm, wot, wq, wk, wv, q, k, v, qbd, wo, sems
):
    groups = 4
    rows = wo.shape[0] // groups
    small = [
        pltpu.make_async_copy(src, dst, sems.at[n])
        for n, (src, dst) in enumerate(((k_hbm, k), (q_hbm, q), (v_hbm, v)))
    ]
    out_copies = []
    for g in range(groups):
        part = pl.ds(g * rows, rows)
        out_copies.append(pltpu.make_async_copy(wo_hbm.at[part], wo.at[part], sems.at[3 + g]))
    others = [
        pltpu.make_async_copy(src, dst, sems.at[3 + groups + n])
        for n, (src, dst) in enumerate(((wk_hbm, wk), (wv_hbm, wv), (wq_hbm, wq)))
    ]
    for copy in small + out_copies + others:
        copy.start()
    qbd[...] = jnp.zeros_like(qbd)
    for copy in small:
        copy.wait()
    for g in range(qbd.shape[0]):
        put_diagonal(qbd, g, q[:, pair_cols(g)])
    for g in range(groups):
        out_copies[g].wait()
        for r in range(0, rows, TILE):
            part = pl.ds(g * rows + r, TILE)
            wot[:, part] = wo[part, :].T
    for copy in others:
        copy.wait()


def prob_kernel(scaling, window, q_ref, k0_ref, k1_ref, k2_ref, pt_ref, kt_ref):
    tile = lax.axis_index("seq")
    odd = lax.rem(tile, 2)
    for g in range(pt_ref.shape[0]):
        for n in range(2):
            h = 2 * g + n
            cols = pl.ds(h * HEAD_DIM, HEAD_DIM)
            q = q_ref[:, cols]
            scores = []
            for b, k_ref in enumerate((k0_ref, k1_ref, k2_ref)):
                k = k_ref[:, cols]
                s = scaling * dot_nt(k, q)
                if b > 0:
                    side = 1 - odd if b == 1 else odd
                    s = jnp.where(window[tile, side, h] > 0, s, -jnp.inf)
                scores.append(s)
                kt_ref[h, :, pl.ds(b * TILE, TILE)] = k.T
            top = jnp.maximum(jnp.maximum(scores[0], scores[1]), scores[2])
            top = jnp.max(top, axis=0, keepdims=True)
            weights = [jnp.exp(s - top) for s in scores]
            total = jnp.sum(weights[0] + weights[1] + weights[2], axis=0, keepdims=True)
            scale = 1.0 / total
            for b, w in enumerate(weights):
                pt_ref[g, pl.ds(b * TILE, TILE), pl.ds(n * TILE, TILE)] = (w * scale).astype(
                    jnp.bfloat16
                )


def cross_kernel(
    scaling, x_ref, wot, qbd, pt, v0, v1, v2, wk, wv, near_ref, far_ref, ds_ref, bd, dk, dv
):
    pairs = pt.shape[0]
    bd[...] = jnp.zeros_like(bd)
    x = x_ref[...]
    for g in range(pairs):
        cols = pair_cols(g)
        put_diagonal(bd, g, dot_nn(x, wot[:, cols]).astype(jnp.bfloat16))
    for g in range(pairs):
        cols = pair_cols(g)
        out = bd[g]
        p = pt[g]
        pf = p.astype(jnp.float32)
        values = jnp.concatenate([v0[:, cols], v1[:, cols], v2[:, cols]], axis=0)
        dp = dot_nt(values, out)
        delta = jnp.sum(pf * dp, axis=0, keepdims=True)
        ds = (pf * ((dp - delta) * scaling)).astype(jnp.bfloat16)
        ds_ref[g] = ds
        dv[:, cols] = dot_nn(p[TILE:], out).astype(jnp.bfloat16)
        dk[:, cols] = dot_nn(ds[TILE:], qbd[g]).astype(jnp.bfloat16)
    step = 768
    for n in range(near_ref.shape[1] // step):
        part = pl.ds(n * step, step)
        cross = dot_nt(dk[...], wk[part, :]) + dot_nt(dv[...], wv[part, :])
        cross = cross.astype(jnp.bfloat16)
        near_ref[:, part] = cross[:TILE]
        far_ref[:, part] = cross[TILE:]


def own_kernel(x_ref, ds_ref, bd, qbd, pt, kt, wq, wk, wv, own_ref, dq, dk, dv):
    for g in range(pt.shape[0]):
        cols = pair_cols(g)
        ds = ds_ref[g]
        dv[:, cols] = dot_nn(pt[g, :TILE], bd[g]).astype(jnp.bfloat16)
        dk[:, cols] = dot_nn(ds[:TILE], qbd[g]).astype(jnp.bfloat16)
        for n in range(2):
            h = 2 * g + n
            dq_t = dot_nn(kt[h], ds[:, n * TILE : (n + 1) * TILE])
            dq[:, pl.ds(h * HEAD_DIM, HEAD_DIM)] = dq_t.T.astype(jnp.bfloat16)
    step = 768
    for n in range(own_ref.shape[1] // step):
        part = pl.ds(n * step, step)
        own_ref[:, part] = (
            dot_nt(dq[...], wq[part, :])
            + dot_nt(dk[...], wk[part, :])
            + dot_nt(dv[...], wv[part, :])
            + x_ref[:, part].astype(jnp.float32)
        )


def sum_kernel(own_ref, near_ref, far_ref, sum_ref):
    total = own_ref[...] + near_ref[...].astype(jnp.float32) + far_ref[...].astype(jnp.float32)
    sum_ref[...] = total.astype(jnp.bfloat16)


def pick_kernel(*refs):
    done_refs, out_ref = refs[:-1], refs[-1]
    position = lax.axis_index("pipe")
    for step, done_ref in enumerate(done_refs):

        @pl.when(position == len(done_refs) - 1 - step)
        def _():
            out_ref[...] = done_ref[...]


def body(
    query_rows,
    key_rows,
    value_rows,
    query_weight,
    key_weight,
    value_weight,
    out_weight,
    upstream,
    window,
):
    sections = lax.axis_size("pipe")
    position = lax.axis_index("pipe")
    seq_size = lax.axis_size("seq")
    seq_index = lax.axis_index("seq")
    rows, width = query_rows.shape[1:]
    model = out_weight.shape[2]
    heads = width // HEAD_DIM
    pairs = heads // 2
    scaling = HEAD_DIM ** (-0.5)
    near_pairs = [(i, i ^ 1) for i in range(seq_size)]
    far_pairs = [(i, i + 1) for i in range(1, seq_size - 1, 2)]
    far_pairs = far_pairs + [(j, i) for i, j in far_pairs]

    def near(value):
        return lax.ppermute(value, "seq", near_pairs)

    def far(value):
        return lax.ppermute(value, "seq", far_pairs)

    k2 = far(key_rows[0])
    v2 = far(value_rows[0])
    k1 = near(key_rows[0])
    v1 = near(value_rows[0])
    vmem = pl.BlockSpec(memory_space=pltpu.VMEM)
    smem = pl.BlockSpec(memory_space=pltpu.SMEM)
    hbm = pl.BlockSpec(memory_space=pltpu.HBM)
    bf16 = jnp.bfloat16

    def params(mib):
        return pltpu.CompilerParams(vmem_limit_bytes=mib * MIB)

    wot, wq, wk, wv, q, k, v, qbd = pl.pallas_call(
        prep_kernel,
        in_specs=[hbm] * 7,
        out_specs=[vmem] * 8,
        out_shape=[
            pltpu.VMEM((model, width), bf16),
            pltpu.VMEM((model, width), bf16),
            pltpu.VMEM((model, width), bf16),
            pltpu.VMEM((model, width), bf16),
            pltpu.VMEM((rows, width), bf16),
            pltpu.VMEM((rows, width), bf16),
            pltpu.VMEM((rows, width), bf16),
            pltpu.VMEM((pairs, 2 * TILE, 2 * HEAD_DIM), bf16),
        ],
        scratch_shapes=[pltpu.VMEM((width, model), bf16), pltpu.SemaphoreType.DMA((10,))],
        compiler_params=params(36),
        name="prep",
    )(
        out_weight[0],
        query_weight[0],
        key_weight[0],
        value_weight[0],
        query_rows[0],
        key_rows[0],
        value_rows[0],
    )
    pt, kt = pl.pallas_call(
        functools.partial(prob_kernel, scaling),
        in_specs=[smem, vmem, vmem, vmem, vmem],
        out_specs=[vmem, vmem],
        out_shape=[
            pltpu.VMEM((pairs, 3 * TILE, 2 * rows), bf16),
            pltpu.VMEM((heads, HEAD_DIM, 3 * TILE), bf16),
        ],
        compiler_params=params(16),
        name="prob",
    )(jnp.transpose(window, (0, 2, 1)), q, k, k1, k2)

    cross = pl.pallas_call(
        functools.partial(cross_kernel, scaling),
        in_specs=[vmem] * 9,
        out_specs=[vmem] * 4,
        out_shape=[
            jax.ShapeDtypeStruct((rows, model), bf16),
            jax.ShapeDtypeStruct((rows, model), bf16),
            pltpu.VMEM((pairs, 3 * TILE, 2 * rows), bf16),
            pltpu.VMEM((pairs, 2 * TILE, 2 * HEAD_DIM), bf16),
        ],
        scratch_shapes=[
            pltpu.VMEM((2 * rows, width), bf16),
            pltpu.VMEM((2 * rows, width), bf16),
        ],
        compiler_params=params(16),
        name="cross",
    )
    own_call = pl.pallas_call(
        own_kernel,
        in_specs=[vmem] * 9,
        out_specs=vmem,
        out_shape=pltpu.VMEM((rows, model), jnp.float32),
        scratch_shapes=[pltpu.VMEM((rows, width), bf16)] * 3,
        compiler_params=params(16),
        name="own",
    )
    add_up = pl.pallas_call(
        sum_kernel,
        in_specs=[vmem] * 3,
        out_specs=vmem,
        out_shape=jax.ShapeDtypeStruct((rows, model), bf16),
        compiler_params=params(16),
        name="add_up",
    )
    pick = pl.pallas_call(
        pick_kernel,
        in_specs=[vmem] * sections,
        out_specs=vmem,
        out_shape=jax.ShapeDtypeStruct((rows, model), bf16),
        compiler_params=params(16),
        name="pick",
    )
    incoming = upstream
    done = []
    for step in range(sections):
        to_near, to_far, ds, bd = cross(incoming, wot, qbd, pt, v, v1, v2, wk, wv)
        from_far = far(to_far)
        from_near = near(to_near)
        own = own_call(incoming, ds, bd, qbd, pt, kt, wq, wk, wv)
        finished = add_up(own, from_near, from_far)
        done.append(finished)
        if step < sections - 1:
            source = sections - 1 - step
            incoming = lax.ppermute(finished, "pipe", [(source, source - 1)])
    return pick(*done)[None]


def solution(mesh):
    in_specs = (
        P("pipe", "seq", None),
        P("pipe", "seq", None),
        P("pipe", "seq", None),
        P("pipe", None, None),
        P("pipe", None, None),
        P("pipe", None, None),
        P("pipe", None, None),
        P("seq", None),
        P(),
    )
    out_specs = P("pipe", "seq", None)
    return jax.shard_map(body, mesh=mesh, in_specs=in_specs, out_specs=out_specs, check_vma=False)
```

time: 149 us -> 113 us (0.76)
  waiting for transfers between devices: 53.4 us -> 31.1 us
  Pallas kernels: 55.8 us -> 50.1 us
  local copies, waits for them, and re-layouts: 5 us -> 0.01 us
    ppermute x6, waiting for transfers between devices: 24 us -> 0.94 us  [far(): return lax.ppermute(value, 'seq', far_pairs)]
    pallas_call x5 -> x15, Pallas kernels: 55.8 us -> 50.1 us  [the longest x4 21.3 us: body(): own = own_call(incoming, ds, bd, qbd, pt, kt, wq, wk, wv)]
    unnamed x14 -> x4, local copies, waits for them, and re-layouts: 4.99 us -> 0.01 us
  transfers between devices with their start and end apart: 15 -> 15, of which waited for: 7 -> 4; matrix products, arithmetic and copies ran while one was open for 0% -> 0% of each run, Pallas kernels for 1% -> 27%
where the time goes in v1:
time: 113 us; the launch traced here: 112 us
  Pallas kernels  50.1 us (44%)
  waiting for transfers between devices  31.1 us (28%)
  starting transfers between devices  30.9 us (27%)
    ppermute x3, waiting for transfers between devices, body(): incoming = lax.ppermute(finished, 'pipe', [(source, source - 1)])  30.2 us
    ppermute x6, starting transfers between devices, far(): return lax.ppermute(value, 'seq', far_pairs)  27.1 us
    pallas_call x4, Pallas kernels, body(): own = own_call(incoming, ds, bd, qbd, pt, kt, wq, wk, wv)  21.3 us
    pallas_call x4, Pallas kernels, body(): to_near, to_far, ds, bd = cross(incoming, wot, qbd, pt, v, v1, v2, wk, wv)  18.7 us
    pallas_call x1, Pallas kernels, body(): pl.pallas_call(prep_kernel, in_specs=[hbm] * 7, out_specs=[vmem] * 8, out...  6.94 us
    ppermute x3, starting transfers between devices, body(): incoming = lax.ppermute(finished, 'pipe', [(source, source - 1)])  2.84 us
  transfers between devices with their start and end apart: 15, of which 4 were waited for; matrix products, arithmetic and copies ran while one was open for 0% of the time, Pallas kernels for 27%

profile of v1, /device:TPU:1, one launch (start us, length us, event | category | flops | bytes accessed | tf_op | source)
XLA Modules:
  0.0 112.5 jit_solution(9502958728412684099)
XLA Ops:
  0.0 4.6 %collective-permute-start.1 = (bf16[128,1536]{1,0:T(8,128)(2,1)}, bf16[128,1536]{1,0:T(8,128)(2,1)S(1)}, u32[]{:S(2)}, u32[]{:S(2)}) collective-permute-start(bf16[128,1536]{1,0:T(8,128)(2,1)} %bitcast.15), channel_id=1, source_target_pairs={{1,2},{3,4},{5,6},{2,1},{4,3},{6,5},{9,10},{11,12},{13,14},{10,9},... | collective-permute-start | bytes 1179656 | tf_op jit(solution)/shard_map/ppermute | solution.py:187
  4.7 3.6 %collective-permute-start.3 = (bf16[128,1536]{1,0:T(8,128)(2,1)}, bf16[128,1536]{1,0:T(8,128)(2,1)S(1)}, u32[]{:S(2)}, u32[]{:S(2)}) collective-permute-start(bf16[128,1536]{1,0:T(8,128)(2,1)} %bitcast.18), channel_id=1, source_target_pairs={{1,2},{3,4},{5,6},{2,1},{4,3},{6,5},{9,10},{11,12},{13,14},{10,9},... | collective-permute-start | bytes 1179656 | tf_op jit(solution)/shard_map/ppermute | solution.py:187
  8.3 6.9 %prep.1 = (bf16[1536,1536]{1,0:T(8,128)(2,1)S(1)}, bf16[1536,1536]{1,0:T(8,128)(2,1)S(1)}, bf16[1536,1536]{1,0:T(8,128)(2,1)S(1)}, bf16[1536,1536]{1,0:T(8,128)(...) custom-call(bf16[1536,1536]{1,0:T(8,128)(2,1)} %bitcast.10, ...), custom_call_target="tpu_custom_call" | custom-call | tf_op jit(solution)/shard_map/prep/pallas_call | solution.py:201
  15.3 2.0 %prob.1 = (bf16[6,384,256]{2,1,0:T(8,128)(2,1)S(1)}, bf16[12,128,384]{2,1,0:T(8,128)(2,1)S(1)}) custom-call(s32[8,2,12]{2,1,0:T(2,128)S(1)} %bitcast.9, bf16[128,1536]{1,0:T(8,128)(2,1)S(1)} %get-tuple-element.33.q_ref, bf16[128,1536]{1,0:T(8,128)(2,1)S(1)} %get-tuple-element.34.k0_ref, bf16[128,1536]{1,0:T(8,128)(2,1)S(1)} %collective-permute-done.k1_ref, ...), custom_call_target="tpu_custom_call" | custom-call | tf_op jit(solution)/shard_map/prob/pallas_call | solution.py:227
  17.4 4.7 %cross.4 = (bf16[128,1536]{1,0:T(8,128)(2,1)S(1)}, bf16[128,1536]{1,0:T(8,128)(2,1)S(1)}, bf16[6,384,256]{2,1,0:T(8,128)(2,1)S(1)}, bf16[6,256,256]{2,1,0:T(8,128)(2,1)S(1)}) custom-call(bf16[128,1536]{1,0:T(8,128)(2,1)S(1)} %copy-done, bf16[1536,1536]{1,0:T(8,128)(2,1)S(1)} %get-tuple-element.31.wot, bf16[6,256,256]{2,1,0:T(8,128)(2,1)S(1)} %get-tuple-element.32.qbd, ...), custom_call_target="tpu_custom_call" | custom-call | tf_op jit(solution)/shard_map/cross/pallas_call | solution.py:284
  22.0 0.5 collective-permute-start.4
  22.6 3.1 %collective-permute-start.5 = (bf16[128,1536]{1,0:T(8,128)(2,1)S(1)}, bf16[128,1536]{1,0:T(8,128)(2,1)S(1)}, u32[]{:S(2)}, u32[]{:S(2)}) collective-permute-start(bf16[128,1536]{1,0:T(8,128)(2,1)S(1)} %get-tuple-element.44), channel_id=1, source_target_pairs={{1,2},{3,4},{5,6},{2,1},{4,3},{6,5},{9,10},{11,12},{13,14},{10,9},... | collective-permute-start | bytes 1179656 | tf_op jit(solution)/shard_map/ppermute | solution.py:187
  25.7 5.3 %own.4.own_ref = f32[128,1536]{1,0:T(8,128)S(1)} custom-call(bf16[128,1536]{1,0:T(8,128)(2,1)S(1)} %copy-done, bf16[6,384,256]{2,1,0:T(8,128)(2,1)S(1)} %get-tuple-element.39.ds_ref, bf16[6,256,256]{2,1,0:T(8,128)(2,1)S(1)} %get-tuple-element.40.bd, bf16[6,256,256]{2,1,0:T(8,128)(2,1)S(1)} %get-tuple-element.32.qbd, ...), custom_call_target="tpu_custom_call" | custom-call | tf_op jit(solution)/shard_map/own/pallas_call | solution.py:287
  31.0 0.6 collective-permute-done.5.far_ref
  31.8 0.9 collective-permute-start.6
  32.7 4.7 %cross.5 = (bf16[128,1536]{1,0:T(8,128)(2,1)S(1)}, bf16[128,1536]{1,0:T(8,128)(2,1)S(1)}, bf16[6,384,256]{2,1,0:T(8,128)(2,1)S(1)}, bf16[6,256,256]{2,1,0:T(8,128)(2,1)S(1)}) custom-call(bf16[128,1536]{1,0:T(8,128)(2,1)S(1)} %collective-permute-done.6.x_ref, bf16[1536,1536]{1,0:T(8,128)(2,1)S(1)} %get-tuple-element.31.wot, ...), custom_call_target="tpu_custom_call" | custom-call | tf_op jit(solution)/shard_map/cross/pallas_call | solution.py:284
  37.4 3.6 %collective-permute-start.8 = (bf16[128,1536]{1,0:T(8,128)(2,1)S(1)}, bf16[128,1536]{1,0:T(8,128)(2,1)S(1)}, u32[]{:S(2)}, u32[]{:S(2)}) collective-permute-start(bf16[128,1536]{1,0:T(8,128)(2,1)S(1)} %get-tuple-element.48), channel_id=1, source_target_pairs={{1,2},{3,4},{5,6},{2,1},{4,3},{6,5},{9,10},{11,12},{13,14},{10,9},... | collective-permute-start | bytes 1179656 | tf_op jit(solution)/shard_map/ppermute | solution.py:187
  41.0 5.3 %own.5.own_ref = f32[128,1536]{1,0:T(8,128)S(1)} custom-call(bf16[128,1536]{1,0:T(8,128)(2,1)S(1)} %collective-permute-done.6.x_ref, bf16[6,384,256]{2,1,0:T(8,128)(2,1)S(1)} %get-tuple-element.45.ds_ref, bf16[6,256,256]{2,1,0:T(8,128)(2,1)S(1)} %get-tuple-element.46.bd, bf16[6,256,256]{2,1,0:T(8,128)(2,1)S(1)} %get-tuple-element.32.qbd, ...), custom_call_target="tpu_custom_call" | custom-call | tf_op jit(solution)/shard_map/own/pallas_call | solution.py:287
  46.4 0.2 collective-permute-done.8.far_ref
  46.7 0.7 collective-permute-start.9
  47.4 4.7 %cross.6 = (bf16[128,1536]{1,0:T(8,128)(2,1)S(1)}, bf16[128,1536]{1,0:T(8,128)(2,1)S(1)}, bf16[6,384,256]{2,1,0:T(8,128)(2,1)S(1)}, bf16[6,256,256]{2,1,0:T(8,128)(2,1)S(1)}) custom-call(bf16[128,1536]{1,0:T(8,128)(2,1)S(1)} %collective-permute-done.9.x_ref, bf16[1536,1536]{1,0:T(8,128)(2,1)S(1)} %get-tuple-element.31.wot, ...), custom_call_target="tpu_custom_call" | custom-call | tf_op jit(solution)/shard_map/cross/pallas_call | solution.py:284
  52.1 3.9 %collective-permute-start.11 = (bf16[128,1536]{1,0:T(8,128)(2,1)S(1)}, bf16[128,1536]{1,0:T(8,128)(2,1)S(1)}, u32[]{:S(2)}, u32[]{:S(2)}) collective-permute-start(bf16[128,1536]{1,0:T(8,128)(2,1)S(1)} %get-tuple-element.52), channel_id=1, source_target_pairs={{1,2},{3,4},{5,6},{2,1},{4,3},{6,5},{9,10},{11,12},{13,14},{10,9},... | collective-permute-start | bytes 1179656 | tf_op jit(solution)/shard_map/ppermute | solution.py:187
  56.0 5.3 %own.6.own_ref = f32[128,1536]{1,0:T(8,128)S(1)} custom-call(bf16[128,1536]{1,0:T(8,128)(2,1)S(1)} %collective-permute-done.9.x_ref, bf16[6,384,256]{2,1,0:T(8,128)(2,1)S(1)} %get-tuple-element.49.ds_ref, bf16[6,256,256]{2,1,0:T(8,128)(2,1)S(1)} %get-tuple-element.50.bd, bf16[6,256,256]{2,1,0:T(8,128)(2,1)S(1)} %get-tuple-element.32.qbd, ...), custom_call_target="tpu_custom_call" | custom-call | tf_op jit(solution)/shard_map/own/pallas_call | solution.py:287
  61.5 1.3 %collective-permute-start.12 = (bf16[128,1536]{1,0:T(8,128)(2,1)S(1)}, bf16[128,1536]{1,0:T(8,128)(2,1)S(1)}, u32[]{:S(2)}, u32[]{:S(2)}) collective-permute-start(bf16[128,1536]{1,0:T(8,128)(2,1)S(1)} %add_up.6.refs_2_), channel_id=1, source_target_pairs={{8,0},{9,1},{10,2},{11,3},{12,4},{13,5},{14,6},{15,7}} | collective-permute-start | bytes 1179656 | tf_op jit(solution)/shard_map/ppermute | solution.py:292
  62.8 30.1 %collective-permute-done.12.x_ref = bf16[128,1536]{1,0:T(8,128)(2,1)S(1)} collective-permute-done((bf16[128,1536]{1,0:T(8,128)(2,1)S(1)}, bf16[128,1536]{1,0:T(8,128)(2,1)S(1)}, u32[]{:S(2)}, u32[]{:S(2)}) %collective-permute-start.12) | collective-permute-done | bytes 393248 | tf_op jit(solution)/shard_map/ppermute | solution.py:292
  92.9 4.7 %cross.7 = (bf16[128,1536]{1,0:T(8,128)(2,1)S(1)}, bf16[128,1536]{1,0:T(8,128)(2,1)S(1)}, bf16[6,384,256]{2,1,0:T(8,128)(2,1)S(1)}, bf16[6,256,256]{2,1,0:T(8,128)(2,1)S(1)}) custom-call(bf16[128,1536]{1,0:T(8,128)(2,1)S(1)} %collective-permute-done.12.x_ref, bf16[1536,1536]{1,0:T(8,128)(2,1)S(1)} %get-tuple-element.31.wot, ...), custom_call_target="tpu_custom_call" | custom-call | tf_op jit(solution)/shard_map/cross/pallas_call | solution.py:284
  97.7 8.4 %collective-permute-start.14 = (bf16[128,1536]{1,0:T(8,128)(2,1)S(1)}, bf16[128,1536]{1,0:T(8,128)(2,1)S(1)}, u32[]{:S(2)}, u32[]{:S(2)}) collective-permute-start(bf16[128,1536]{1,0:T(8,128)(2,1)S(1)} %get-tuple-element.56), channel_id=1, source_target_pairs={{1,2},{3,4},{5,6},{2,1},{4,3},{6,5},{9,10},{11,12},{13,14},{10,9},... | collective-permute-start | bytes 1179656 | tf_op jit(solution)/shard_map/ppermute | solution.py:187
  106.1 5.3 %own.7.own_ref = f32[128,1536]{1,0:T(8,128)S(1)} custom-call(bf16[128,1536]{1,0:T(8,128)(2,1)S(1)} %collective-permute-done.12.x_ref, bf16[6,384,256]{2,1,0:T(8,128)(2,1)S(1)} %get-tuple-element.53.ds_ref, bf16[6,256,256]{2,1,0:T(8,128)(2,1)S(1)} %get-tuple-element.54.bd, bf16[6,256,256]{2,1,0:T(8,128)(2,1)S(1)} %get-tuple-element.32.qbd, ...), custom_call_target="tpu_custom_call" | custom-call | tf_op jit(solution)/shard_map/own/pallas_call | solution.py:287
  111.7 0.8 pick.1
  (25 shorter events, 1.0 us)
Async XLA Ops:
  0.0 15.3 %collective-permute-start.1 = (bf16[128,1536]{1,0:T(8,128)(2,1)}, bf16[128,1536]{1,0:T(8,128)(2,1)S(1)}, u32[]{:S(2)}, u32[]{:S(2)}) collective-permute-start(bf16[128,1536]{1,0:T(8,128)(2,1)} %bitcast.15), channel_id=1, source_target_pairs={{1,2},{3,4},{5,6},{2,1},{4,3},{6,5},{9,10},{11,12},{13,14},{10,9},... | collective-permute-start | bytes 1179656 | tf_op jit(solution)/shard_map/ppermute | solution.py:187
  4.6 10.7 %collective-permute-start = (bf16[128,1536]{1,0:T(8,128)(2,1)}, bf16[128,1536]{1,0:T(8,128)(2,1)S(1)}, u32[]{:S(2)}, u32[]{:S(2)}) collective-permute-start(bf16[128,1536]{1,0:T(8,128)(2,1)} %bitcast.16), channel_id=1, source_target_pairs={{0,1},{1,0},{2,3},{3,2},{4,5},{5,4},{6,7},{7,6},{8,9},{9,8},{10,11... | collective-permute-start | bytes 1179656 | tf_op jit(solution)/shard_map/ppermute | solution.py:184
  4.7 12.7 %collective-permute-start.3 = (bf16[128,1536]{1,0:T(8,128)(2,1)}, bf16[128,1536]{1,0:T(8,128)(2,1)S(1)}, u32[]{:S(2)}, u32[]{:S(2)}) collective-permute-start(bf16[128,1536]{1,0:T(8,128)(2,1)} %bitcast.18), channel_id=1, source_target_pairs={{1,2},{3,4},{5,6},{2,1},{4,3},{6,5},{9,10},{11,12},{13,14},{10,9},... | collective-permute-start | bytes 1179656 | tf_op jit(solution)/shard_map/ppermute | solution.py:187
  8.3 9.1 %collective-permute-start.2 = (bf16[128,1536]{1,0:T(8,128)(2,1)}, bf16[128,1536]{1,0:T(8,128)(2,1)S(1)}, u32[]{:S(2)}, u32[]{:S(2)}) collective-permute-start(bf16[128,1536]{1,0:T(8,128)(2,1)} %bitcast.19), channel_id=1, source_target_pairs={{0,1},{1,0},{2,3},{3,2},{4,5},{5,4},{6,7},{7,6},{8,9},{9,8},{10,11... | collective-permute-start | bytes 1179656 | tf_op jit(solution)/shard_map/ppermute | solution.py:184
  8.3 7.0 %copy-start.1 = (s32[8,12,2]{1,2,0:T(2,128)S(1)}, s32[8,12,2]{1,2,0:T(2,128)}, u32[]{:S(2)}) copy-start(s32[8,12,2]{1,2,0:T(2,128)} %param.17) | copy-start | bytes 2308
  8.3 9.0 %copy-start = (bf16[128,1536]{1,0:T(8,128)(2,1)S(1)}, bf16[128,1536]{1,0:T(8,128)(2,1)}, u32[]{:S(2)}) copy-start(bf16[128,1536]{1,0:T(8,128)(2,1)} %x_ref.3) | copy-start | bytes 1179652
  22.0 9.0 %collective-permute-start.4 = (bf16[128,1536]{1,0:T(8,128)(2,1)S(1)}, bf16[128,1536]{1,0:T(8,128)(2,1)S(1)}, u32[]{:S(2)}, u32[]{:S(2)}) collective-permute-start(bf16[128,1536]{1,0:T(8,128)(2,1)S(1)} %get-tuple-element.43), channel_id=1, source_target_pairs={{0,1},{1,0},{2,3},{3,2},{4,5},{5,4},{6,7},{7,6},{8,9},{9,8},{10,11... | collective-permute-start | bytes 1179656 | tf_op jit(solution)/shard_map/ppermute | solution.py:184
  22.6 9.1 %collective-permute-start.5 = (bf16[128,1536]{1,0:T(8,128)(2,1)S(1)}, bf16[128,1536]{1,0:T(8,128)(2,1)S(1)}, u32[]{:S(2)}, u32[]{:S(2)}) collective-permute-start(bf16[128,1536]{1,0:T(8,128)(2,1)S(1)} %get-tuple-element.44), channel_id=1, source_target_pairs={{1,2},{3,4},{5,6},{2,1},{4,3},{6,5},{9,10},{11,12},{13,14},{10,9},... | collective-permute-start | bytes 1179656 | tf_op jit(solution)/shard_map/ppermute | solution.py:187
  31.8 0.9 collective-permute-start.6
  37.4 9.0 %collective-permute-start.7 = (bf16[128,1536]{1,0:T(8,128)(2,1)S(1)}, bf16[128,1536]{1,0:T(8,128)(2,1)S(1)}, u32[]{:S(2)}, u32[]{:S(2)}) collective-permute-start(bf16[128,1536]{1,0:T(8,128)(2,1)S(1)} %get-tuple-element.47), channel_id=1, source_target_pairs={{0,1},{1,0},{2,3},{3,2},{4,5},{5,4},{6,7},{7,6},{8,9},{9,8},{10,11... | collective-permute-start | bytes 1179656 | tf_op jit(solution)/shard_map/ppermute | solution.py:184
  37.4 9.1 %collective-permute-start.8 = (bf16[128,1536]{1,0:T(8,128)(2,1)S(1)}, bf16[128,1536]{1,0:T(8,128)(2,1)S(1)}, u32[]{:S(2)}, u32[]{:S(2)}) collective-permute-start(bf16[128,1536]{1,0:T(8,128)(2,1)S(1)} %get-tuple-element.48), channel_id=1, source_target_pairs={{1,2},{3,4},{5,6},{2,1},{4,3},{6,5},{9,10},{11,12},{13,14},{10,9},... | collective-permute-start | bytes 1179656 | tf_op jit(solution)/shard_map/ppermute | solution.py:187
  46.7 0.7 collective-permute-start.9
  52.0 9.3 %collective-permute-start.10 = (bf16[128,1536]{1,0:T(8,128)(2,1)S(1)}, bf16[128,1536]{1,0:T(8,128)(2,1)S(1)}, u32[]{:S(2)}, u32[]{:S(2)}) collective-permute-start(bf16[128,1536]{1,0:T(8,128)(2,1)S(1)} %get-tuple-element.51), channel_id=1, source_target_pairs={{0,1},{1,0},{2,3},{3,2},{4,5},{5,4},{6,7},{7,6},{8,9},{9,8},{10,11... | collective-permute-start | bytes 1179656 | tf_op jit(solution)/shard_map/ppermute | solution.py:184
  52.1 9.2 %collective-permute-start.11 = (bf16[128,1536]{1,0:T(8,128)(2,1)S(1)}, bf16[128,1536]{1,0:T(8,128)(2,1)S(1)}, u32[]{:S(2)}, u32[]{:S(2)}) collective-permute-start(bf16[128,1536]{1,0:T(8,128)(2,1)S(1)} %get-tuple-element.52), channel_id=1, source_target_pairs={{1,2},{3,4},{5,6},{2,1},{4,3},{6,5},{9,10},{11,12},{13,14},{10,9},... | collective-permute-start | bytes 1179656 | tf_op jit(solution)/shard_map/ppermute | solution.py:187
  61.5 31.4 %collective-permute-start.12 = (bf16[128,1536]{1,0:T(8,128)(2,1)S(1)}, bf16[128,1536]{1,0:T(8,128)(2,1)S(1)}, u32[]{:S(2)}, u32[]{:S(2)}) collective-permute-start(bf16[128,1536]{1,0:T(8,128)(2,1)S(1)} %add_up.6.refs_2_), channel_id=1, source_target_pairs={{8,0},{9,1},{10,2},{11,3},{12,4},{13,5},{14,6},{15,7}} | collective-permute-start | bytes 1179656 | tf_op jit(solution)/shard_map/ppermute | solution.py:292
  97.6 13.8 %collective-permute-start.13 = (bf16[128,1536]{1,0:T(8,128)(2,1)S(1)}, bf16[128,1536]{1,0:T(8,128)(2,1)S(1)}, u32[]{:S(2)}, u32[]{:S(2)}) collective-permute-start(bf16[128,1536]{1,0:T(8,128)(2,1)S(1)} %get-tuple-element.55), channel_id=1, source_target_pairs={{0,1},{1,0},{2,3},{3,2},{4,5},{5,4},{6,7},{7,6},{8,9},{9,8},{10,11... | collective-permute-start | bytes 1179656 | tf_op jit(solution)/shard_map/ppermute | solution.py:184
  97.7 13.8 %collective-permute-start.14 = (bf16[128,1536]{1,0:T(8,128)(2,1)S(1)}, bf16[128,1536]{1,0:T(8,128)(2,1)S(1)}, u32[]{:S(2)}, u32[]{:S(2)}) collective-permute-start(bf16[128,1536]{1,0:T(8,128)(2,1)S(1)} %get-tuple-element.56), channel_id=1, source_target_pairs={{1,2},{3,4},{5,6},{2,1},{4,3},{6,5},{9,10},{11,12},{13,14},{10,9},... | collective-permute-start | bytes 1179656 | tf_op jit(solution)/shard_map/ppermute | solution.py:187
